TPU v7x, 32 devices: a whole 2x2x4 slice. The times are simulated.
32 devices in a mesh: seq: 16 (over z, x, core), row: 2 (over y).
Axes of the slice: x: 2, y: 2, z: 4, core: 2. Of those that a mesh axis runs over, the one named last changes fastest.
Arguments:
- queries: bfloat16 [2, 16, 128, 3072], P(None, 'seq', 'row'), may hold values from -9 to 9
- keys: bfloat16 [2, 16, 128, 512], P(None, 'seq', 'row'), may hold values from -9 to 9
- values: bfloat16 [2, 16, 128, 512], P(None, 'seq', 'row'), may hold values from -6 to 6
- gain: float32 [128], replicated, may hold values from 0.1 to 1.9
Outputs:
- attended: bfloat16 [2, 16, 128, 3072], P(None, 'seq', 'row')
All inputs are finite; a program needn't handle non-finite values.
Results may differ from a plain program's by a relative error of at most 0.017.
Values may be sent and summed in bfloat16 or wider, within the bound.
A program may use at most 128 MiB of HBM per device.

v0:
```python
import math

import jax
import jax.numpy as jnp
from jax import lax
from jax.sharding import PartitionSpec as P

KV_HEADS = 4
GROUP = 6
HEAD_DIM = 128


lowest_score = -1e30


def attend_block(state, query_group, key_block, value_block, visible):
    running_max, running_sum, running_acc = state
    scores = jnp.einsum(
        "qgjd,kgd->qgjk", query_group, key_block, preferred_element_type=jnp.float32
    )
    scores = scores * (1.0 / math.sqrt(HEAD_DIM))
    scores = jnp.where(visible, scores, -jnp.inf)
    new_max = jnp.maximum(running_max, jnp.max(scores, axis=-1))
    raw_weights = jnp.exp(scores - new_max[..., None])
    factor = jnp.exp(running_max - new_max)
    new_sum = running_sum * factor + jnp.sum(raw_weights, axis=-1)
    weights = raw_weights.astype(jnp.bfloat16)
    new_acc = running_acc * factor[..., None] + jnp.einsum(
        "qgjk,kgd->qgjd", weights, value_block, preferred_element_type=jnp.float32
    )
    return (new_max, new_sum, new_acc)


def fold_history(queries_here, query_blocks, keys_here, values_here):
    query_count = queries_here.shape[2]
    key_rows = keys_here.shape[2]
    block_count = 2 * lax.axis_size("seq")
    grouped = queries_here.reshape(2, query_count, KV_HEADS, GROUP, HEAD_DIM)
    stat_shape = (2, query_count, KV_HEADS, GROUP)
    initial = (
        jnp.full(stat_shape, lowest_score, jnp.float32),
        jnp.zeros(stat_shape, jnp.float32),
        jnp.zeros(stat_shape + (HEAD_DIM,), jnp.float32),
    )
    key_piece = lax.all_gather(keys_here, "seq", axis=1, tiled=True)
    value_piece = lax.all_gather(values_here, "seq", axis=1, tiled=True)
    shard_count = key_piece.shape[1]
    per_step = math.gcd(shard_count, max(1, 1024 // key_rows))
    step_count = shard_count // per_step
    span_rows = per_step * key_rows
    key_blocks = key_piece.reshape(2 * step_count, span_rows, KV_HEADS, HEAD_DIM)
    value_blocks = value_piece.reshape(2 * step_count, span_rows, KV_HEADS, HEAD_DIM)
    step_ids = jnp.arange(2 * step_count, dtype=jnp.int32)
    shard_of_row = jnp.arange(span_rows, dtype=jnp.int32) // key_rows

    def visit(state, operands):
        key_block, value_block, step_id = operands
        which_half = step_id // step_count
        device_ids = step_id % step_count * per_step + shard_of_row
        key_ids = jnp.where(which_half == 0, device_ids, block_count - 1 - device_ids)
        updated = []
        for query_half in range(2):
            current = (state[0][query_half], state[1][query_half], state[2][query_half])
            visible = key_ids <= query_blocks[query_half]
            current = attend_block(current, grouped[query_half], key_block, value_block, visible)
            updated.append(current)
        new_state = (
            jnp.stack([updated[0][0], updated[1][0]]),
            jnp.stack([updated[0][1], updated[1][1]]),
            jnp.stack([updated[0][2], updated[1][2]]),
        )
        return (new_state, None)

    result_state, _ = lax.scan(visit, initial, (key_blocks, value_blocks, step_ids))
    return result_state


def per_device(queries, keys, values, gain):
    seq_index = lax.axis_index("seq")
    block_count = 2 * lax.axis_size("seq")
    query_blocks = jnp.stack([seq_index, block_count - 1 - seq_index])
    own_rows = queries.shape[2]
    keys_here, values_here = (
        lax.all_gather(keys, "row", axis=2, tiled=True),
        lax.all_gather(values, "row", axis=2, tiled=True),
    )
    running_max, running_sum, running_acc = fold_history(
        queries, query_blocks, keys_here, values_here
    )
    mixed = running_acc / running_sum[..., None]
    spread = jnp.sqrt(jnp.mean(mixed * mixed, axis=-1, keepdims=True) + 1e-06)
    normed = (mixed / spread * gain).astype(jnp.bfloat16)
    return normed.reshape(2, 1, own_rows, KV_HEADS * GROUP * HEAD_DIM)


def solution(mesh):
    return jax.shard_map(
        per_device,
        mesh=mesh,
        in_specs=(
            P(None, "seq", "row", None),
            P(None, "seq", "row", None),
            P(None, "seq", "row", None),
            P(),
        ),
        out_specs=P(None, "seq", "row", None),
        check_vma=False,
    )
```

profile of v0, /device:TPU:0, one launch (start us, length us, event | category | flops | bytes accessed | tf_op | source)
XLA Modules:
  0.0 193.1 jit_solution(7251539220374075740)
XLA Ops:
  6.5 9.0 %all_gather.12 = bf16[2,1,128,512]{3,2,1,0:T(8,128)(2,1)} all-gather(bf16[2,1,64,512]{3,2,1,0:T(8,128)(2,1)} %param.7), channel_id=1, replica_groups=mesh['seq'=16,'row'=2] {'row'}, dimensions={2}, use_global_device_ids=true | all-gather | bytes 393216 | tf_op jit(solution)/shard_map/all_gather | solution.py:84
  15.6 6.0 %all_gather.14 = bf16[2,1,128,512]{3,2,1,0:T(8,128)(2,1)} all-gather(bf16[2,1,64,512]{3,2,1,0:T(8,128)(2,1)} %param.8), channel_id=1, replica_groups=mesh['seq'=16,'row'=2] {'row'}, dimensions={2}, use_global_device_ids=true | all-gather | bytes 393216 | tf_op jit(solution)/shard_map/all_gather | solution.py:85
  21.6 2.1 %reshape.97 = bf16[2,64,4,6,128]{4,3,2,1,0:T(8,128)(2,1)S(1)} reshape(bf16[2,1,64,3072]{3,2,1,0:T(8,128)(2,1)} %param.6) | data formatting | bytes 1572864 | tf_op jit(solution)/shard_map/reshape | solution.py:38
  23.6 0.3 copy.7
  24.0 42.6 %all-gather.3.cloned.1.call-done = bf16[2,16,128,512]{3,2,1,0:T(8,128)(2,1)} async-done(((bf16[2,1,128,512]{3,2,1,0:T(8,128)(2,1)}), bf16[2,16,128,512]{3,2,1,0:T(8,128)(2,1)}) %all-gather.3.cloned.1.call-update) | async-done | bytes 4194320 | tf_op jit(solution)/shard_map/all_gather | solution.py:45
  66.6 6.9 %reshape.96 = bf16[4,1024,4,128]{3,2,1,0:T(4,128)(2,1)} reshape(bf16[2,16,128,512]{3,2,1,0:T(8,128)(2,1)} %all-gather.3.cloned.1.call-done) | data formatting | bytes 8388608 | tf_op jit(solution)/shard_map/reshape | solution.py:51
  73.5 44.4 %all-gather.5.cloned.1.call-done = bf16[2,16,128,512]{3,2,1,0:T(8,128)(2,1)} async-done(((bf16[2,1,128,512]{3,2,1,0:T(8,128)(2,1)}), bf16[2,16,128,512]{3,2,1,0:T(8,128)(2,1)}) %all-gather.5.cloned.1.call-update) | async-done | bytes 4194320 | tf_op jit(solution)/shard_map/all_gather | solution.py:46
  117.9 6.9 %reshape.98 = bf16[4,1024,4,128]{3,2,1,0:T(4,128)(2,1)} reshape(bf16[2,16,128,512]{3,2,1,0:T(8,128)(2,1)} %all-gather.5.cloned.1.call-done) | data formatting | bytes 8388608 | tf_op jit(solution)/shard_map/reshape | solution.py:52
  124.8 0.2 broadcast_in_dim.39
  125.0 57.6 %while.17 = (s32[]{:T(128)}, f32[2,64,4,6]{1,3,2,0:T(8,128)S(1)}, f32[2,64,4,6]{1,3,2,0:T(8,128)S(1)}, f32[2,64,4,6,128]{4,1,3,2,0:T(8,128)S(1)}, s32[4]{0:T(128...) while((s32[]{:T(128)}, f32[2,64,4,6]{1,3,2,0:T(8,128)S(1)}, ...), condition=%wide.region_5.6_spmd.clone, body=%wide.region_0.5_spmd.clone.sunk | while | flops 1646427136 | bytes 53457280 | solution.py:74
  125.0 0.6 dynamic_slice.28
  127.9 2.3 %constant_dynamic-slice_fusion.3 = (bf16[1,1024,4,128]{3,2,1,0:T(4,128)(2,1)S(1)}, bf16[1,1024,4,128]{3,2,1,0:T(4,128)(2,1)S(1)}) fusion(bf16[4,1024,4,128]{3,2,1,0:T(4,128)(2,1)} %get-tuple-element.352, s32[]{:T(128)S(6)} %copy.37, bf16[4,1024,4,128]{3,2,1,0:T(4,128)(2,1)} %get-tuple-element.349), kind=kLoop, calls=%fused_computation.57.clone.1 | loop fusion | bytes 4194308 | tf_op jit(solution)/shard_map/while/body/jit(dynamic_index_in_dim)/dynamic_slice | solution.py:74
  130.1 1.1 bitcast_reduce_fusion.5
  131.2 1.1 bitcast_reduce_fusion.4
  132.3 1.6 fusion.62
  133.9 1.8 fusion.65
  135.7 1.8 fusion.64
  137.5 1.6 fusion.63
  139.3 0.6 dynamic_slice.28
  142.2 2.3 %constant_dynamic-slice_fusion.3 = (bf16[1,1024,4,128]{3,2,1,0:T(4,128)(2,1)S(1)}, bf16[1,1024,4,128]{3,2,1,0:T(4,128)(2,1)S(1)}) fusion(bf16[4,1024,4,128]{3,2,1,0:T(4,128)(2,1)} %get-tuple-element.352, s32[]{:T(128)S(6)} %copy.37, bf16[4,1024,4,128]{3,2,1,0:T(4,128)(2,1)} %get-tuple-element.349), kind=kLoop, calls=%fused_computation.57.clone.1 | loop fusion | bytes 4194308 | tf_op jit(solution)/shard_map/while/body/jit(dynamic_index_in_dim)/dynamic_slice | solution.py:74
  144.5 1.1 bitcast_reduce_fusion.5
  145.6 1.1 bitcast_reduce_fusion.4
  146.7 1.6 fusion.62
  148.2 1.8 fusion.65
  150.1 1.8 fusion.64
  151.9 1.6 fusion.63
  153.4 0.2 pad_maximum_fusion.8
  153.7 0.6 dynamic_slice.28
  156.6 2.3 %constant_dynamic-slice_fusion.3 = (bf16[1,1024,4,128]{3,2,1,0:T(4,128)(2,1)S(1)}, bf16[1,1024,4,128]{3,2,1,0:T(4,128)(2,1)S(1)}) fusion(bf16[4,1024,4,128]{3,2,1,0:T(4,128)(2,1)} %get-tuple-element.352, s32[]{:T(128)S(6)} %copy.37, bf16[4,1024,4,128]{3,2,1,0:T(4,128)(2,1)} %get-tuple-element.349), kind=kLoop, calls=%fused_computation.57.clone.1 | loop fusion | bytes 4194308 | tf_op jit(solution)/shard_map/while/body/jit(dynamic_index_in_dim)/dynamic_slice | solution.py:74
  158.8 1.1 bitcast_reduce_fusion.5
  159.9 1.1 bitcast_reduce_fusion.4
  161.0 1.6 fusion.62
  162.6 1.8 fusion.65
  164.4 1.8 fusion.64
  166.2 1.6 fusion.63
  167.8 0.2 pad_maximum_fusion.8
  168.0 0.6 dynamic_slice.28
  170.9 2.3 %constant_dynamic-slice_fusion.3 = (bf16[1,1024,4,128]{3,2,1,0:T(4,128)(2,1)S(1)}, bf16[1,1024,4,128]{3,2,1,0:T(4,128)(2,1)S(1)}) fusion(bf16[4,1024,4,128]{3,2,1,0:T(4,128)(2,1)} %get-tuple-element.352, s32[]{:T(128)S(6)} %copy.37, bf16[4,1024,4,128]{3,2,1,0:T(4,128)(2,1)} %get-tuple-element.349), kind=kLoop, calls=%fused_computation.57.clone.1 | loop fusion | bytes 4194308 | tf_op jit(solution)/shard_map/while/body/jit(dynamic_index_in_dim)/dynamic_slice | solution.py:74
  173.2 1.1 bitcast_reduce_fusion.5
  174.3 1.1 bitcast_reduce_fusion.4
  175.4 1.6 fusion.62
  176.9 1.8 fusion.65
  178.8 1.8 fusion.64
  180.6 1.6 fusion.63
  182.6 0.9 multiply_reduce_fusion
  183.5 0.5 multiply_convert_fusion
  184.0 0.5 copy.9
  184.6 1.7 reshape.99
  (32 shorter events, 0.7 us)
Async XLA Ops:
  6.5 60.0 %all-gather.3.cloned.1.call-start = ((), (), s32[]{:S(2)}) async-start(), calls=%async_computation | async-start | bytes 4456448 | tf_op jit(solution)/shard_map/all_gather | solution.py:45
  15.5 102.3 %all-gather.5.cloned.1.call-start = ((), (), s32[]{:S(2)}) async-start(), calls=%async_computation.1 | async-start | bytes 4456448 | tf_op jit(solution)/shard_map/all_gather | solution.py:46
  125.0 58.5 %copy-start = (f32[128]{0:T(128)S(1)}, f32[128]{0:T(128)}, u32[]{:S(2)}) copy-start(f32[128]{0:T(128)} %param.9) | copy-start | bytes 1540
Sparse Core Ops, SparseCore 0:
  15.7 50.8 all-gather.2
  68.7 49.0 all-gather.4
where the time goes:
time: 194 us; the launch traced here: 193 us
  waiting for transfers between devices  87 us (45%)
  local copies, waits for them, and re-layouts  30 us (15%)
  matrix products  23.2 us (12%)
  blocking collectives  14.9 us (8%)
  other arithmetic  14.7 us (8%)
  between operations  13.5 us (7%)
  loops' own time  9.75 us (5%)
    all_gather x1, waiting for transfers between devices, fold_history(): value_piece = lax.all_gather(values_here, 'seq', axis=1, tiled=True)  44.4 us
    all_gather x1, waiting for transfers between devices, fold_history(): key_piece = lax.all_gather(keys_here, 'seq', axis=1, tiled=True)  42.6 us
    dot_general x8, matrix products, attend_block(): jnp.einsum('qgjk,kgd->qgjd', weights, value_block, preferred_element_type...  14.5 us
    reduce_sum x8, other arithmetic, attend_block(): new_sum = running_sum * factor + jnp.sum(raw_weights, axis=-1)  12.4 us
    dynamic_slice x8, local copies, waits for them, and re-layouts, fold_history(): lax.scan(visit, initial, (key_blocks, value_blocks, step_ids))  11.3 us
    another operation x1, loops' own time, fold_history(): lax.scan(visit, initial, (key_blocks, value_blocks, step_ids))  9.75 us
    all_gather x1, blocking collectives, per_device(): lax.all_gather(keys, 'row', axis=2, tiled=True)  8.97 us
    dot_general x8, matrix products, attend_block(): jnp.einsum('qgjd,kgd->qgjk', query_group, key_block, preferred_element_ty...  8.64 us
  transfers between devices with their start and end apart: 2, of which 2 were waited for; matrix products, arithmetic and copies ran while one was open for 5% of the time, Pallas kernels for 0%

commit v1 on v0

v1 whole, which is shorter than its diff:
```python
import functools
import math

import jax
import jax.numpy as jnp
from jax import lax
from jax.experimental import pallas as pl
from jax.experimental.pallas import tpu as pltpu
from jax.sharding import PartitionSpec as P

KV_HEADS = 4
GROUP = 6
HEAD_DIM = 128
LOWEST = -1e30
EXPONENT = math.log2(math.e) / math.sqrt(HEAD_DIM)

DOWN, UP, ACROSS_X, ACROSS_Y, CORE = range(5)


def kernel(planes, q_ref, k_ref, v_ref, gain_ref, out_ref, qs, buf, top, total, acc,
           local_sem, send_sem, recv_sem):
    seq = lax.axis_index("seq")
    y = lax.axis_index("row")
    z, x, c = seq // 4, (seq // 2) % 2, seq % 2
    own_group = seq // 2
    rows = q_ref.shape[2]
    other_y = 1 - y
    devices = {
        DOWN: {"seq": seq - 4},
        UP: {"seq": seq + 4},
        ACROSS_X: {"seq": seq + 2 - 4 * x},
        ACROSS_Y: {"row": other_y},
        CORE: {"seq": seq + 1 - 2 * c},
    }

    load_k = pltpu.make_async_copy(k_ref.at[:, 0], buf.at[0, :, own_group, c, y], local_sem.at[0])
    load_v = pltpu.make_async_copy(v_ref.at[:, 0], buf.at[1, :, own_group, c, y], local_sem.at[1])
    load_k.start()
    load_v.start()

    barrier = pltpu.get_barrier_semaphore()

    def greet(where):
        pl.semaphore_signal(barrier, inc=1, device_id=devices[where],
                            device_id_type=pl.DeviceIdType.MESH)

    has_down, has_up = z > 0, z < planes - 1
    pl.when(has_down)(lambda: greet(DOWN))
    pl.when(has_up)(lambda: greet(UP))
    for where in (ACROSS_X, ACROSS_Y, CORE):
        greet(where)
    pl.semaphore_wait(barrier, 3 + has_down.astype(jnp.int32) + has_up.astype(jnp.int32))

    def piece(group, core, row, half, where):
        ref = buf.at[:, half, group, core, row]
        return pltpu.make_async_remote_copy(
            src_ref=ref, dst_ref=ref,
            send_sem=send_sem.at[group, row, half, where],
            recv_sem=recv_sem.at[group, core, row, half],
            device_id=devices[where], device_id_type=pl.DeviceIdType.MESH)

    def start(copy):
        copy.start()

    def finish(copy):
        copy.wait_send()

    def arrived(group, core, row, half):
        piece(group, core, row, half, CORE).wait_recv()

    def column(plane, act, wait):
        group = 2 * plane + x

        def visit(half):
            if wait:
                arrived(group, c, y, half)
            pl.when(has_down & (plane >= z))(lambda: act(piece(group, c, y, half, DOWN)))
            if half == 0:
                pl.when(has_up & (plane <= z))(lambda: act(piece(group, c, y, half, UP)))
            for where in (ACROSS_X, ACROSS_Y, CORE):
                act(piece(group, c, y, half, where))

        visit(0)
        pl.when(plane >= z)(lambda: visit(1))

    def sides(plane, act, wait):
        def visit(half):
            for across, group, row in ((0, 2 * plane + 1 - x, y), (1, 2 * plane + x, other_y)):
                if wait:
                    arrived(group, c, row, half)
                if across == half:
                    act(piece(group, c, row, half, ACROSS_X if across else ACROSS_Y))
                act(piece(group, c, row, half, CORE))

        visit(0)
        pl.when(plane >= z)(lambda: visit(1))

    def corner(plane, act, wait):
        group = 2 * plane + 1 - x

        def visit(half):
            if wait:
                arrived(group, c, other_y, half)
            act(piece(group, c, other_y, half, CORE))

        visit(0)
        pl.when(plane >= z)(lambda: visit(1))

    def from_core(plane):
        def visit(half):
            for dx in range(2):
                for dy in range(2):
                    arrived(2 * plane + dx, 1 - c, dy, half)

        visit(0)
        pl.when(plane >= z)(lambda: visit(1))

    def attend(query_half, kv_refs):
        for head in range(KV_HEADS):
            lanes = slice(head * HEAD_DIM, (head + 1) * HEAD_DIM)
            key = kv_refs[0][..., lanes].reshape(-1, HEAD_DIM)
            value = kv_refs[1][..., lanes].reshape(-1, HEAD_DIM)
            scores = lax.dot_general(key, qs[query_half, head], (((1,), (1,)), ((), ())),
                                     preferred_element_type=jnp.float32)
            old = top[query_half, head]
            new = jnp.maximum(old, jnp.max(scores, axis=0, keepdims=True))
            weights = jnp.exp2((scores - new) * EXPONENT)
            factor = jnp.exp2((old - new) * EXPONENT)
            top[query_half, head] = new
            total[query_half, head] = total[query_half, head] * factor + jnp.sum(
                weights, axis=0, keepdims=True)
            acc[query_half, head] = acc[query_half, head] * factor + lax.dot_general(
                value.T, weights.astype(jnp.bfloat16), (((1,), (0,)), ((), ())),
                preferred_element_type=jnp.float32)

    def attend_plane(plane):
        @pl.loop(0, 4)
        def _(i):
            group = 2 * plane + i // 2
            second = i % 2
            above = (group > own_group).astype(jnp.int32)
            query_half = 1 - second * (1 - above)
            key_half = second * above

            @pl.when((second == 0) | (group != own_group))
            def _():
                attend(query_half, (buf.at[0, key_half, group], buf.at[1, key_half, group]))

    def attend_own():
        @pl.loop(0, 3)
        def _(i):
            last = i // 2
            core = c + last * (1 - 2 * c)
            half = (i % 2) * (1 - last) + last * (1 - c)
            attend(half, (buf.at[0, half, own_group, core], buf.at[1, half, own_group, core]))

    load_k.wait()
    load_v.wait()
    column(z, start, False)

    for half in range(2):
        for head in range(KV_HEADS * GROUP):
            at = (head % GROUP) * rows
            qs[half, head // GROUP, at:at + rows, :] = q_ref[
                half, 0, :, head * HEAD_DIM:(head + 1) * HEAD_DIM]
    top[...] = jnp.full(top.shape, LOWEST, jnp.float32)
    total[...] = jnp.zeros(total.shape, jnp.float32)
    acc[...] = jnp.zeros(acc.shape, jnp.float32)

    @pl.loop(0, planes)
    def _(step):
        @pl.loop(0, 2)
        def _(way):
            plane = z + (step + 1) * (1 - 2 * way)

            @pl.when((plane >= 0) & (plane < planes))
            def _():
                column(plane, start, True)

        @pl.loop(0, 2)
        def _(way):
            plane = z + step * (1 - 2 * way)

            @pl.when((plane >= 0) & (plane < planes) & ((way == 0) | (step > 0)))
            def _():
                sides(plane, start, True)
                corner(plane, start, True)
                from_core(plane)
                pl.when(step == 0)(attend_own)
                attend_plane(plane)

    for half in range(2):
        for kv_head in range(KV_HEADS):
            mixed = acc[half, kv_head] / total[half, kv_head]
            spread = jnp.sqrt(jnp.mean(mixed * mixed, axis=0, keepdims=True) + 1e-06)
            normed = (mixed / spread * gain_ref[...]).T.astype(jnp.bfloat16)
            for member in range(GROUP):
                head = kv_head * GROUP + member
                out_ref[half, 0, :, head * HEAD_DIM:(head + 1) * HEAD_DIM] = normed[
                    member * rows:(member + 1) * rows]

    @pl.loop(0, planes)
    def _(plane):
        column(plane, finish, False)
        sides(plane, finish, False)
        corner(plane, finish, False)


def per_device(queries, keys, values, gain):
    seq_size = lax.axis_size("seq")
    planes = seq_size // 4
    rows, width = keys.shape[2], keys.shape[3]
    stacked = GROUP * rows
    buf_shape = (2, 2, 2 * planes, 2, 2, rows, width)
    buf_bytes = 2 * math.prod(buf_shape)
    vmem = pl.BlockSpec(memory_space=pltpu.VMEM)
    units = 2 * (2 * seq_size + 1) * rows * 2 * rows
    return pl.pallas_call(
        functools.partial(kernel, planes),
        out_shape=jax.ShapeDtypeStruct(queries.shape, jnp.bfloat16),
        in_specs=[vmem, pl.BlockSpec(memory_space=pl.ANY), pl.BlockSpec(memory_space=pl.ANY), vmem],
        out_specs=vmem,
        scratch_shapes=[
            pltpu.VMEM((2, KV_HEADS, stacked, HEAD_DIM), jnp.bfloat16),
            pltpu.VMEM(buf_shape, jnp.bfloat16),
            pltpu.VMEM((2, KV_HEADS, 1, stacked), jnp.float32),
            pltpu.VMEM((2, KV_HEADS, 1, stacked), jnp.float32),
            pltpu.VMEM((2, KV_HEADS, HEAD_DIM, stacked), jnp.float32),
            pltpu.SemaphoreType.DMA((2,)),
            pltpu.SemaphoreType.DMA((2 * planes, 2, 2, 5)),
            pltpu.SemaphoreType.DMA((2 * planes, 2, 2, 2)),
        ],
        compiler_params=pltpu.CompilerParams(
            collective_id=0, has_side_effects=True, vmem_limit_bytes=buf_bytes + 14 * 2**20
        ),
        cost_estimate=pl.CostEstimate(
            flops=units * KV_HEADS * GROUP * HEAD_DIM * 2,
            bytes_accessed=2 * queries.size * 2,
            transcendentals=units * KV_HEADS * GROUP // 2),
    )(queries, keys, values, gain.reshape(HEAD_DIM, 1))


def solution(mesh):
    return jax.shard_map(
        per_device,
        mesh=mesh,
        in_specs=(
            P(None, "seq", "row", None),
            P(None, "seq", "row", None),
            P(None, "seq", "row", None),
            P(),
        ),
        out_specs=P(None, "seq", "row", None),
        check_vma=False,
    )
```

time: 194 us -> 81.1 us (0.42)
  waiting for transfers between devices: 87 us -> 0 us
  Pallas kernels: 0 us -> 76.3 us
  local copies, waits for them, and re-layouts: 30 us -> 4.59 us
  matrix products: 23.2 us -> 0 us
  blocking collectives: 14.9 us -> 0 us
  other arithmetic: 14.7 us -> 0 us
  between operations: 13.5 us -> 0.02 us
  loops' own time: 9.75 us -> 0 us
    all_gather x2 -> x0, waiting for transfers between devices: 87 us -> none  [the longest x1 44.4 us: fold_history(): value_piece = lax.all_gather(values_here, 'seq', axis=1, tiled=True)]
    pallas_call x0 -> x1, Pallas kernels: none -> 76.3 us  [per_device(): pl.pallas_call(functools.partial(kernel, planes), out_shape=jax.ShapeDtyp...]
    dot_general x16 -> x0, matrix products: 23.2 us -> none  [the longest x8 14.5 us: attend_block(): jnp.einsum('qgjk,kgd->qgjd', weights, value_block, preferred_element_type...]
    reshape x4 -> x1, local copies, waits for them, and re-layouts: 17.6 us -> 0.11 us  [per_device(): gain.reshape(HEAD_DIM, 1)]
    all_gather x2 -> x0, blocking collectives: 14.9 us -> none  [the longest x1 8.97 us: per_device(): lax.all_gather(keys, 'row', axis=2, tiled=True)]
    reduce_sum x9 -> x0, other arithmetic: 13.3 us -> none  [the longest x8 12.4 us: attend_block(): new_sum = running_sum * factor + jnp.sum(raw_weights, axis=-1)]
    dynamic_slice x8 -> x0, local copies, waits for them, and re-layouts: 11.3 us -> none  [fold_history(): lax.scan(visit, initial, (key_blocks, value_blocks, step_ids))]
    another operation x1 -> x0, loops' own time: 9.75 us -> none  [fold_history(): lax.scan(visit, initial, (key_blocks, value_blocks, step_ids))]
  transfers between devices with their start and end apart: 2 -> 0, of which waited for: 2 -> 0; matrix products, arithmetic and copies ran while one was open for 5% -> 0% of each run, Pallas kernels for 0% -> 0%
where the time goes in v1:
time: 81.1 us; the launch traced here: 80.9 us
  Pallas kernels  76.3 us (94%)
  local copies, waits for them, and re-layouts  4.59 us (6%)
    pallas_call x1, Pallas kernels, per_device(): pl.pallas_call(functools.partial(kernel, planes), out_shape=jax.ShapeDtyp...  76.3 us
    unnamed x9, local copies, waits for them, and re-layouts  4.47 us

profile of v1, /device:TPU:0, one launch (start us, length us, event | category | flops | bytes accessed | tf_op | source)
XLA Modules:
  0.0 80.9 jit_solution(4670605946206510505)
XLA Ops:
  0.0 0.0 copy-start.3
  0.0 0.7 copy-done.3
  0.7 0.1 copy.5.gain_ref
  0.8 0.0 copy-start
  0.8 1.1 %copy-done = bf16[2,1,64,3072]{3,2,1,0:T(8,128)(2,1)S(1)} copy-done((bf16[2,1,64,3072]{3,2,1,0:T(8,128)(2,1)S(1)}, bf16[2,1,64,3072]{3,2,1,0:T(8,128)(2,1)}, u32[]{:S(2)}) %copy-start) | copy-done | bytes 786456
  1.9 0.0 copy-start.1
  1.9 0.9 %copy-done.1 = bf16[2,1,64,512]{3,2,1,0:T(8,128)(2,1)S(1)} copy-done((bf16[2,1,64,512]{3,2,1,0:T(8,128)(2,1)S(1)}, bf16[2,1,64,512]{3,2,1,0:T(8,128)(2,1)}, u32[]{:S(2)}) %copy-start.1) | copy-done | bytes 131096
  2.8 0.0 copy-start.2
  2.8 0.9 %copy-done.2 = bf16[2,1,64,512]{3,2,1,0:T(8,128)(2,1)S(1)} copy-done((bf16[2,1,64,512]{3,2,1,0:T(8,128)(2,1)S(1)}, bf16[2,1,64,512]{3,2,1,0:T(8,128)(2,1)}, u32[]{:S(2)}) %copy-start.2) | copy-done | bytes 131096
  3.7 76.3 %shard_map.46 = bf16[2,1,64,3072]{3,2,1,0:T(8,128)(2,1)S(1)} custom-call(bf16[2,1,64,3072]{3,2,1,0:T(8,128)(2,1)S(1)} %copy-done, bf16[2,1,64,512]{3,2,1,0:T(8,128)(2,1)S(1)} %copy-done.1, bf16[2,1,64,512]{3,2,1,0:T(8,128)(2,1)S(1)} %copy-done.2, f32[128,1]{1,0:T(8,128)S(1)} %copy.5.gain_ref), custom_call_target="tpu_custom_call" | custom-call | flops 3321888768 | bytes 1572864 | tf_op jit(solution)/shard_map/pallas_call | solution.py:218
  80.0 0.9 %copy.7 = bf16[2,1,64,3072]{3,2,1,0:T(8,128)(2,1)} copy(bf16[2,1,64,3072]{3,2,1,0:T(8,128)(2,1)S(1)} %shard_map.46) | data formatting | bytes 1572864
Async XLA Ops:
  0.0 0.7 copy-start.3
  0.8 1.1 %copy-start = (bf16[2,1,64,3072]{3,2,1,0:T(8,128)(2,1)S(1)}, bf16[2,1,64,3072]{3,2,1,0:T(8,128)(2,1)}, u32[]{:S(2)}) copy-start(bf16[2,1,64,3072]{3,2,1,0:T(8,128)(2,1)} %q_ref.1) | copy-start | bytes 2359300
  1.9 0.9 %copy-start.1 = (bf16[2,1,64,512]{3,2,1,0:T(8,128)(2,1)S(1)}, bf16[2,1,64,512]{3,2,1,0:T(8,128)(2,1)}, u32[]{:S(2)}) copy-start(bf16[2,1,64,512]{3,2,1,0:T(8,128)(2,1)} %k_ref.1) | copy-start | bytes 393220
  2.8 0.9 %copy-start.2 = (bf16[2,1,64,512]{3,2,1,0:T(8,128)(2,1)S(1)}, bf16[2,1,64,512]{3,2,1,0:T(8,128)(2,1)}, u32[]{:S(2)}) copy-start(bf16[2,1,64,512]{3,2,1,0:T(8,128)(2,1)} %v_ref.1) | copy-start | bytes 393220

commit v2 on v1

--- a/solution.py
+++ b/solution.py
@@ -17,7 +17,7 @@
 DOWN, UP, ACROSS_X, ACROSS_Y, CORE = range(5)
 
 
-def kernel(planes, q_ref, k_ref, v_ref, gain_ref, out_ref, qs, buf, top, total, acc,
+def kernel(planes, q_hbm, k_ref, v_ref, gain_ref, out_ref, q_ref, qs, buf, top, total, acc,
            local_sem, send_sem, recv_sem):
     seq = lax.axis_index("seq")
     y = lax.axis_index("row")
@@ -37,6 +37,8 @@
     load_v = pltpu.make_async_copy(v_ref.at[:, 0], buf.at[1, :, own_group, c, y], local_sem.at[1])
     load_k.start()
     load_v.start()
+    load_q = pltpu.make_async_copy(q_hbm, q_ref, local_sem.at[2])
+    load_q.start()
 
     barrier = pltpu.get_barrier_semaphore()
 
@@ -116,22 +118,25 @@
         pl.when(plane >= z)(lambda: visit(1))
 
     def attend(query_half, kv_refs):
-        for head in range(KV_HEADS):
-            lanes = slice(head * HEAD_DIM, (head + 1) * HEAD_DIM)
-            key = kv_refs[0][..., lanes].reshape(-1, HEAD_DIM)
-            value = kv_refs[1][..., lanes].reshape(-1, HEAD_DIM)
-            scores = lax.dot_general(key, qs[query_half, head], (((1,), (1,)), ((), ())),
-                                     preferred_element_type=jnp.float32)
-            old = top[query_half, head]
-            new = jnp.maximum(old, jnp.max(scores, axis=0, keepdims=True))
-            weights = jnp.exp2((scores - new) * EXPONENT)
-            factor = jnp.exp2((old - new) * EXPONENT)
-            top[query_half, head] = new
-            total[query_half, head] = total[query_half, head] * factor + jnp.sum(
-                weights, axis=0, keepdims=True)
-            acc[query_half, head] = acc[query_half, head] * factor + lax.dot_general(
-                value.T, weights.astype(jnp.bfloat16), (((1,), (0,)), ((), ())),
-                preferred_element_type=jnp.float32)
+        heads = range(KV_HEADS)
+        cut = [slice(h * HEAD_DIM, (h + 1) * HEAD_DIM) for h in heads]
+        old = [top[query_half, h] for h in heads]
+        old_total = [total[query_half, h] for h in heads]
+        scores = [lax.dot_general(kv_refs[0][..., cut[h]].reshape(-1, HEAD_DIM), qs[query_half, h],
+                                  (((1,), (1,)), ((), ())),
+                                  preferred_element_type=jnp.float32) for h in heads]
+        new = [jnp.maximum(old[h], jnp.max(scores[h], axis=0, keepdims=True)) for h in heads]
+        weights = [jnp.exp2((scores[h] - new[h]) * EXPONENT) for h in heads]
+        factor = [jnp.exp2((old[h] - new[h]) * EXPONENT) for h in heads]
+        added = [jnp.sum(weights[h], axis=0, keepdims=True) for h in heads]
+        mixed = [lax.dot_general(
+            kv_refs[1][..., cut[h]].reshape(-1, HEAD_DIM).T, weights[h].astype(jnp.bfloat16),
+            (((1,), (0,)), ((), ())), preferred_element_type=jnp.float32) for h in heads]
+        old_acc = [acc[query_half, h] for h in heads]
+        for h in heads:
+            top[query_half, h] = new[h]
+            total[query_half, h] = old_total[h] * factor[h] + added[h]
+            acc[query_half, h] = old_acc[h] * factor[h] + mixed[h]
 
     def attend_plane(plane):
         @pl.loop(0, 4)
@@ -157,6 +162,7 @@
     load_k.wait()
     load_v.wait()
     column(z, start, False)
+    load_q.wait()
 
     for half in range(2):
         for head in range(KV_HEADS * GROUP):
@@ -167,33 +173,38 @@
     total[...] = jnp.zeros(total.shape, jnp.float32)
     acc[...] = jnp.zeros(acc.shape, jnp.float32)
 
-    @pl.loop(0, planes)
+    def at_distance(distance, visit):
+        @pl.when((distance >= 0) & (distance < planes))
+        def _():
+            @pl.loop(0, 2)
+            def _(way):
+                plane = z + distance * (1 - 2 * way)
+                pl.when((plane >= 0) & (plane < planes) & ((way == 0) | (distance > 0)))(
+                    lambda: visit(plane))
+
+    def pass_on_column(plane):
+        pl.when(plane != z)(lambda: column(plane, start, True))
+
+    def take_rest(plane):
+        corner(plane, start, True)
+        from_core(plane)
+
+    def compute(plane):
+        pl.when(plane == z)(attend_own)
+        attend_plane(plane)
+
+    @pl.loop(0, planes + 2)
     def _(step):
-        @pl.loop(0, 2)
-        def _(way):
-            plane = z + (step + 1) * (1 - 2 * way)
-
-            @pl.when((plane >= 0) & (plane < planes))
-            def _():
-                column(plane, start, True)
-
-        @pl.loop(0, 2)
-        def _(way):
-            plane = z + step * (1 - 2 * way)
-
-            @pl.when((plane >= 0) & (plane < planes) & ((way == 0) | (step > 0)))
-            def _():
-                sides(plane, start, True)
-                corner(plane, start, True)
-                from_core(plane)
-                pl.when(step == 0)(attend_own)
-                attend_plane(plane)
+        at_distance(step, pass_on_column)
+        at_distance(step - 1, lambda plane: sides(plane, start, True))
+        at_distance(step - 2, take_rest)
+        at_distance(step - 2, compute)
 
     for half in range(2):
         for kv_head in range(KV_HEADS):
             mixed = acc[half, kv_head] / total[half, kv_head]
             spread = jnp.sqrt(jnp.mean(mixed * mixed, axis=0, keepdims=True) + 1e-06)
-            normed = (mixed / spread * gain_ref[...]).T.astype(jnp.bfloat16)
+            normed = ((mixed / spread).T * gain_ref[...]).astype(jnp.bfloat16)
             for member in range(GROUP):
                 head = kv_head * GROUP + member
                 out_ref[half, 0, :, head * HEAD_DIM:(head + 1) * HEAD_DIM] = normed[
@@ -212,32 +223,32 @@
     rows, width = keys.shape[2], keys.shape[3]
     stacked = GROUP * rows
     buf_shape = (2, 2, 2 * planes, 2, 2, rows, width)
-    buf_bytes = 2 * math.prod(buf_shape)
     vmem = pl.BlockSpec(memory_space=pltpu.VMEM)
     units = 2 * (2 * seq_size + 1) * rows * 2 * rows
     return pl.pallas_call(
         functools.partial(kernel, planes),
         out_shape=jax.ShapeDtypeStruct(queries.shape, jnp.bfloat16),
-        in_specs=[vmem, pl.BlockSpec(memory_space=pl.ANY), pl.BlockSpec(memory_space=pl.ANY), vmem],
+        in_specs=[pl.BlockSpec(memory_space=pltpu.HBM)] * 3 + [vmem],
         out_specs=vmem,
         scratch_shapes=[
+            pltpu.VMEM(queries.shape, jnp.bfloat16),
             pltpu.VMEM((2, KV_HEADS, stacked, HEAD_DIM), jnp.bfloat16),
             pltpu.VMEM(buf_shape, jnp.bfloat16),
             pltpu.VMEM((2, KV_HEADS, 1, stacked), jnp.float32),
             pltpu.VMEM((2, KV_HEADS, 1, stacked), jnp.float32),
             pltpu.VMEM((2, KV_HEADS, HEAD_DIM, stacked), jnp.float32),
-            pltpu.SemaphoreType.DMA((2,)),
+            pltpu.SemaphoreType.DMA((3,)),
             pltpu.SemaphoreType.DMA((2 * planes, 2, 2, 5)),
             pltpu.SemaphoreType.DMA((2 * planes, 2, 2, 2)),
         ],
         compiler_params=pltpu.CompilerParams(
-            collective_id=0, has_side_effects=True, vmem_limit_bytes=buf_bytes + 14 * 2**20
+            collective_id=0, has_side_effects=True, vmem_limit_bytes=56 * 2**20
         ),
         cost_estimate=pl.CostEstimate(
             flops=units * KV_HEADS * GROUP * HEAD_DIM * 2,
             bytes_accessed=2 * queries.size * 2,
             transcendentals=units * KV_HEADS * GROUP // 2),
-    )(queries, keys, values, gain.reshape(HEAD_DIM, 1))
+    )(queries, keys, values, gain.reshape(1, HEAD_DIM))
 
 
 def solution(mesh):

time: 81.1 us -> 52.4 us (0.65); the launches traced: 80.9 us -> 51.4 us
  Pallas kernels: 76.3 us -> 49.3 us
  local copies, waits for them, and re-layouts: 4.59 us -> 2.06 us
    pallas_call x1, Pallas kernels: 76.3 us -> 49.3 us  [per_device(): pl.pallas_call(functools.partial(kernel, planes), out_shape=jax.ShapeDtyp...]
    unnamed x9 -> x1, local copies, waits for them, and re-layouts: 4.47 us -> 2.06 us
where the time goes in v2:
time: 52.4 us; the launch traced here: 51.4 us
  Pallas kernels  49.3 us (94%)
  local copies, waits for them, and re-layouts  2.06 us (4%)
    pallas_call x1, Pallas kernels, per_device(): pl.pallas_call(functools.partial(kernel, planes), out_shape=jax.ShapeDtyp...  49.3 us
    unnamed x1, local copies, waits for them, and re-layouts  2.06 us

profile of v2, /device:TPU:0, one launch (start us, length us, event | category | flops | bytes accessed | tf_op | source)
XLA Modules:
  0.0 51.4 jit_solution(2674717733630391819)
XLA Ops:
  0.0 49.3 %shard_map.46 = bf16[2,1,64,3072]{3,2,1,0:T(8,128)(2,1)} custom-call(bf16[2,1,64,3072]{3,2,1,0:T(8,128)(2,1)} %q_hbm.1, bf16[2,1,64,512]{3,2,1,0:T(8,128)(2,1)} %k_ref.1, bf16[2,1,64,512]{3,2,1,0:T(8,128)(2,1)} %v_ref.1, f32[1,128]{1,0:T(1,128)} %bitcast.1), custom_call_target="tpu_custom_call" | custom-call | flops 3321888768 | bytes 1572864 | tf_op jit(solution)/shard_map/pallas_call | solution.py:228
  49.3 2.1 %copy.6 = bf16[2,1,64,3072]{3,2,1,0:T(8,128)(2,1)} copy(bf16[2,1,64,3072]{3,2,1,0:T(8,128)(2,1)} %shard_map.46) | data formatting | bytes 1572864

commit v3 on v2

v3 whole, which is shorter than its diff:
```python
import functools
import math

import jax
import jax.numpy as jnp
from jax import lax
from jax.experimental import pallas as pl
from jax.experimental.pallas import tpu as pltpu
from jax.sharding import PartitionSpec as P

KV_HEADS = 4
GROUP = 6
HEAD_DIM = 128
LOWEST = -1e30
EXPONENT = math.log2(math.e) / math.sqrt(HEAD_DIM)

KV_HERE = KV_HEADS // 2
KV_WIDTH = KV_HERE * HEAD_DIM
HEAD_WIDTH = GROUP * HEAD_DIM
Q_WIDTH = KV_HERE * HEAD_WIDTH

DOWN, UP, ACROSS_X, CORE = range(4)
MESH = pl.DeviceIdType.MESH


def kernel(planes, q_ref, k_ref, v_ref, gain_ref, out_ref, q_all, qs, buf, top, total, acc, made,
           local_sem, swap_send, swap_recv, keep_sem, back_send, back_recv, send_sem, recv_sem):
    seq = lax.axis_index("seq")
    y = lax.axis_index("row")
    z, x, c = seq // 4, (seq // 2) % 2, seq % 2
    own_group = seq // 2
    rows = q_all.shape[2]
    other_y = 1 - y
    devices = {
        DOWN: {"seq": seq - 4},
        UP: {"seq": seq + 4},
        ACROSS_X: {"seq": seq + 2 - 4 * x},
        CORE: {"seq": seq + 1 - 2 * c},
    }
    partner = {"row": other_y}

    def columns(which, width):
        return pl.ds(pl.multiple_of(which * width, width), width)

    sources = ((k_ref, buf.at[0, :, own_group, c, y], KV_WIDTH),
               (v_ref, buf.at[1, :, own_group, c, y], KV_WIDTH),
               (q_ref, q_all.at[:, y], Q_WIDTH))
    loads = [pltpu.make_async_copy(ref.at[:, 0, :, columns(y, width)], to, local_sem.at[i])
             for i, (ref, to, width) in enumerate(sources)]
    swaps = [pltpu.make_async_remote_copy(
        src_ref=ref.at[:, 0, :, columns(other_y, width)], dst_ref=to,
        send_sem=swap_send.at[i], recv_sem=swap_recv.at[i],
        device_id=partner, device_id_type=MESH) for i, (ref, to, width) in enumerate(sources)]
    for load in loads:
        load.start()

    barrier = pltpu.get_barrier_semaphore()

    def greet(device):
        pl.semaphore_signal(barrier, inc=1, device_id=device, device_id_type=MESH)

    has_down, has_up = z > 0, z < planes - 1
    pl.when(has_down)(lambda: greet(devices[DOWN]))
    pl.when(has_up)(lambda: greet(devices[UP]))
    for device in (devices[ACROSS_X], devices[CORE], partner):
        greet(device)
    pl.semaphore_wait(barrier, 3 + has_down.astype(jnp.int32) + has_up.astype(jnp.int32))

    def piece(group, core, row, half, where):
        ref = buf.at[:, half, group, core, row]
        return pltpu.make_async_remote_copy(
            src_ref=ref, dst_ref=ref,
            send_sem=send_sem.at[group, row, half, where],
            recv_sem=recv_sem.at[group, core, row, half],
            device_id=devices[where], device_id_type=MESH)

    def start(copy):
        copy.start()

    def finish(copy):
        copy.wait_send()

    def arrived(group, core, row, half):
        piece(group, core, row, half, CORE).wait_recv()

    def column_row(plane, row, act, wait):
        group = 2 * plane + x

        def visit(half):
            if wait:
                arrived(group, c, row, half)
            pl.when(has_down & (plane >= z))(lambda: act(piece(group, c, row, half, DOWN)))
            if half == 0:
                pl.when(has_up & (plane <= z))(lambda: act(piece(group, c, row, half, UP)))
            act(piece(group, c, row, half, ACROSS_X))
            act(piece(group, c, row, half, CORE))

        visit(0)
        pl.when(plane >= z)(lambda: visit(1))

    def column(plane, act, wait):
        column_row(plane, y, act, wait)
        column_row(plane, other_y, act, wait)

    def side(plane, act, wait):
        group = 2 * plane + 1 - x

        def visit(half):
            for row in (y, other_y):
                if wait:
                    arrived(group, c, row, half)
                act(piece(group, c, row, half, CORE))

        visit(0)
        pl.when(plane >= z)(lambda: visit(1))

    def from_core(plane):
        def visit(half):
            for dx in range(2):
                for dy in range(2):
                    arrived(2 * plane + dx, 1 - c, dy, half)

        visit(0)
        pl.when(plane >= z)(lambda: visit(1))

    def attend(query_half, kv_refs):
        heads = range(KV_HERE)
        cut = [slice(h * HEAD_DIM, (h + 1) * HEAD_DIM) for h in heads]
        old = [top[query_half, h] for h in heads]
        old_total = [total[query_half, h] for h in heads]
        scores = [lax.dot_general(kv_refs[0][..., cut[h]].reshape(-1, HEAD_DIM), qs[query_half, h],
                                  (((1,), (1,)), ((), ())),
                                  preferred_element_type=jnp.float32) for h in heads]
        new = [jnp.maximum(old[h], jnp.max(scores[h], axis=0, keepdims=True)) for h in heads]
        weights = [jnp.exp2((scores[h] - new[h]) * EXPONENT) for h in heads]
        factor = [jnp.exp2((old[h] - new[h]) * EXPONENT) for h in heads]
        added = [jnp.sum(weights[h], axis=0, keepdims=True) for h in heads]
        mixed = [lax.dot_general(
            kv_refs[1][..., cut[h]].reshape(-1, HEAD_DIM).T, weights[h].astype(jnp.bfloat16),
            (((1,), (0,)), ((), ())), preferred_element_type=jnp.float32) for h in heads]
        old_acc = [acc[query_half, h] for h in heads]
        for h in heads:
            top[query_half, h] = new[h]
            total[query_half, h] = old_total[h] * factor[h] + added[h]
            acc[query_half, h] = old_acc[h] * factor[h] + mixed[h]

    def attend_plane(plane):
        @pl.loop(0, 4)
        def _(i):
            group = 2 * plane + i // 2
            second = i % 2
            above = (group > own_group).astype(jnp.int32)
            query_half = 1 - second * (1 - above)
            key_half = second * above

            @pl.when((second == 0) | (group != own_group))
            def _():
                attend(query_half, (buf.at[0, key_half, group], buf.at[1, key_half, group]))

    def attend_own():
        @pl.loop(0, 3)
        def _(i):
            last = i // 2
            core = c + last * (1 - 2 * c)
            half = (i % 2) * (1 - last) + last * (1 - c)
            attend(half, (buf.at[0, half, own_group, core], buf.at[1, half, own_group, core]))

    def result_copies(half, kv_head):
        here = pl.ds(kv_head * HEAD_WIDTH, HEAD_WIDTH)
        there = out_ref.at[half, 0, :, columns(y * KV_HERE + kv_head, HEAD_WIDTH)]
        keep = pltpu.make_async_copy(made.at[half, y, :, here], there, keep_sem.at[half, kv_head])
        back = pltpu.make_async_remote_copy(
            src_ref=made.at[half, other_y, :, here], dst_ref=there,
            send_sem=back_send.at[half, kv_head], recv_sem=back_recv.at[half, kv_head],
            device_id=partner, device_id_type=MESH)
        return keep, back

    def emit(half):
        for kv_head in range(KV_HERE):
            mixed = acc[half, kv_head] / total[half, kv_head]
            spread = jnp.sqrt(jnp.mean(mixed * mixed, axis=0, keepdims=True) + 1e-06)
            normed = ((mixed / spread).T * gain_ref[...]).astype(jnp.bfloat16)
            for member in range(GROUP):
                lane = (kv_head * GROUP + member) * HEAD_DIM
                for row in range(2):
                    at = (2 * member + row) * rows
                    made[half, row, :, lane:lane + HEAD_DIM] = normed[at:at + rows]
            keep, back = result_copies(half, kv_head)
            back.start()
            keep.start()

    swaps[0].start()
    swaps[1].start()
    loads[0].wait()
    loads[1].wait()
    column_row(z, y, start, False)
    top[...] = jnp.full(top.shape, LOWEST, jnp.float32)
    total[...] = jnp.zeros(total.shape, jnp.float32)
    acc[...] = jnp.zeros(acc.shape, jnp.float32)
    swaps[0].wait_recv()
    swaps[1].wait_recv()
    column_row(z, other_y, start, False)
    swaps[2].start()

    def at_distance(distance, visit):
        @pl.when((distance >= 0) & (distance < planes))
        def _():
            @pl.loop(0, 2)
            def _(way):
                plane = z + distance * (1 - 2 * way)
                pl.when((plane >= 0) & (plane < planes) & ((way == 0) | (distance > 0)))(
                    lambda: visit(plane))

    def take_queries():
        loads[2].wait()
        swaps[2].wait_recv()
        for half in range(2):
            for head in range(KV_HERE * GROUP):
                for row in range(2):
                    at = (2 * (head % GROUP) + row) * rows
                    qs[half, head // GROUP, at:at + rows, :] = q_all[
                        half, row, :, head * HEAD_DIM:(head + 1) * HEAD_DIM]

    def pass_on_column(plane):
        pl.when(plane != z)(lambda: column(plane, start, True))

    def compute(plane):
        from_core(plane)

        @pl.when(plane == z)
        def _():
            take_queries()
            attend_own()

        attend_plane(plane)

    @pl.loop(0, planes + 2)
    def _(step):
        at_distance(step, pass_on_column)
        at_distance(step - 2, compute)
        pl.when(step - 2 == z)(lambda: emit(0))
        at_distance(step - 1, lambda plane: side(plane, start, True))

    emit(1)

    @pl.loop(0, planes)
    def _(plane):
        column(plane, finish, False)
        side(plane, finish, False)

    for swap in swaps:
        swap.wait_send()
    for half in range(2):
        for kv_head in range(KV_HERE):
            keep, back = result_copies(half, kv_head)
            keep.wait()
            back.wait()


def per_device(queries, keys, values, gain):
    seq_size = lax.axis_size("seq")
    planes = seq_size // 4
    rows = keys.shape[2]
    stacked = GROUP * 2 * rows
    hbm = pl.BlockSpec(memory_space=pltpu.HBM)
    units = 2 * (2 * seq_size + 1) * rows * 2 * rows
    return pl.pallas_call(
        functools.partial(kernel, planes),
        out_shape=jax.ShapeDtypeStruct(queries.shape, jnp.bfloat16),
        in_specs=[hbm, hbm, hbm, pl.BlockSpec(memory_space=pltpu.VMEM)],
        out_specs=hbm,
        scratch_shapes=[
            pltpu.VMEM((2, 2, rows, Q_WIDTH), jnp.bfloat16),
            pltpu.VMEM((2, KV_HERE, stacked, HEAD_DIM), jnp.bfloat16),
            pltpu.VMEM((2, 2, 2 * planes, 2, 2, rows, KV_WIDTH), jnp.bfloat16),
            pltpu.VMEM((2, KV_HERE, 1, stacked), jnp.float32),
            pltpu.VMEM((2, KV_HERE, 1, stacked), jnp.float32),
            pltpu.VMEM((2, KV_HERE, HEAD_DIM, stacked), jnp.float32),
            pltpu.VMEM((2, 2, rows, Q_WIDTH), jnp.bfloat16),
            pltpu.SemaphoreType.DMA((3,)),
            pltpu.SemaphoreType.DMA((3,)),
            pltpu.SemaphoreType.DMA((3,)),
            pltpu.SemaphoreType.DMA((2, KV_HERE)),
            pltpu.SemaphoreType.DMA((2, KV_HERE)),
            pltpu.SemaphoreType.DMA((2, KV_HERE)),
            pltpu.SemaphoreType.DMA((2 * planes, 2, 2, 4)),
            pltpu.SemaphoreType.DMA((2 * planes, 2, 2, 2)),
        ],
        compiler_params=pltpu.CompilerParams(
            collective_id=0, has_side_effects=True, vmem_limit_bytes=56 * 2**20
        ),
        cost_estimate=pl.CostEstimate(
            flops=units * KV_HEADS * GROUP * HEAD_DIM * 2,
            bytes_accessed=2 * queries.size * 2,
            transcendentals=units * KV_HEADS * GROUP // 2),
    )(queries, keys, values, gain.reshape(1, HEAD_DIM))


def solution(mesh):
    return jax.shard_map(
        per_device,
        mesh=mesh,
        in_specs=(
            P(None, "seq", "row", None),
            P(None, "seq", "row", None),
            P(None, "seq", "row", None),
            P(),
        ),
        out_specs=P(None, "seq", "row", None),
        check_vma=False,
    )
```

time: 52.4 us -> 50.2 us (0.958)
  Pallas kernels: 49.3 us -> 47.3 us
    pallas_call x1, Pallas kernels: 49.3 us -> 47.3 us  [per_device(): pl.pallas_call(functools.partial(kernel, planes), out_shape=jax.ShapeDtyp...]
where the time goes in v3:
time: 50.2 us; the launch traced here: 49.4 us
  Pallas kernels  47.3 us (94%)
  local copies, waits for them, and re-layouts  2.06 us (4%)
    pallas_call x1, Pallas kernels, per_device(): pl.pallas_call(functools.partial(kernel, planes), out_shape=jax.ShapeDtyp...  47.3 us
    unnamed x1, local copies, waits for them, and re-layouts  2.06 us

profile of v3, /device:TPU:0, one launch (start us, length us, event | category | flops | bytes accessed | tf_op | source)
XLA Modules:
  0.0 49.4 jit_solution(13250889593132444432)
XLA Ops:
  0.0 47.3 %shard_map.46 = bf16[2,1,64,3072]{3,2,1,0:T(8,128)(2,1)} custom-call(bf16[2,1,64,3072]{3,2,1,0:T(8,128)(2,1)} %q_ref.1, bf16[2,1,64,512]{3,2,1,0:T(8,128)(2,1)} %k_ref.1, bf16[2,1,64,512]{3,2,1,0:T(8,128)(2,1)} %v_ref.1, f32[1,128]{1,0:T(1,128)} %bitcast.1), custom_call_target="tpu_custom_call" | custom-call | flops 3321888768 | bytes 1572864 | tf_op jit(solution)/shard_map/pallas_call | solution.py:267
  47.3 2.1 %copy.6 = bf16[2,1,64,3072]{3,2,1,0:T(8,128)(2,1)} copy(bf16[2,1,64,3072]{3,2,1,0:T(8,128)(2,1)} %shard_map.46) | data formatting | bytes 1572864
